TPU v7x, 256 devices: a whole 4x4x8 slice. The times are simulated.
256 devices in a mesh: tm: 8 (over z), tile: 32 (over x, y, core).
Axes of the slice: x: 4, y: 4, z: 8, core: 2. Of those that a mesh axis runs over, the one named last changes fastest.
Arguments:
- latents: bfloat16 [32, 16, 16, 256], P('tile', 'tm'), may hold values from -6 to 6
- writer: int32 [32], replicated, may hold values from 0 to 31, as said below
- margin_cols: int32 [32], P('tile'), may hold values from 0 to 4, as said below
- in_weight: bfloat16 [3, 144, 512], replicated, may hold values from -0.3125 to 0.3125
- in_bias: float32 [512], replicated, may hold values from -3 to 3
- mid_weight: bfloat16 [3, 4608, 256], replicated, may hold values from -0.0546875 to 0.0546875
- mid_bias: float32 [256], replicated, may hold values from -3 to 3
- skip_weight: bfloat16 [512, 256], replicated, may hold values from -0.25 to 0.25
- head_weight: bfloat16 [256, 3], replicated, may hold values from -0.375 to 0.375
- head_bias: float32 [3], replicated, may hold values from -3 to 3
Outputs:
- written: bfloat16 [96, 16, 3, 256], P('tile', 'tm')
- blended: bfloat16 [32, 16, 3, 256], P('tile', 'tm')
Inputs may be any that keep to these rules, and one draw needn't show every extreme that they name: `writer`: each device of tile is named at most 3 times, and one device exactly 3 times. `margin_cols`: 0 where a tile starts a clip, always for tile 0; otherwise from 2 to 4.
All inputs are finite; a program needn't handle non-finite values.
Results may differ from a plain program's by a relative error of at most 0.015.
Values may be sent and summed in bfloat16 or wider, within the bound.
A program may use at most 128 MiB of HBM per device.

v0:
```python
import jax
import jax.numpy as jnp
from jax import lax
from jax.sharding import PartitionSpec as P

TH = 16
TW = 16
MAXLOAD = 3
MARGIN_HI = 4


def from_behind(block, axis, distance):
    devices = range(lax.axis_size(axis))
    route = [(i - distance, i) for i in devices if i - distance in devices]
    return lax.ppermute(block, axis, route)


def shift_pixels(values, row_step, col_step):
    if row_step < 0:
        values = jnp.concatenate([values[..., :TW], values[..., :-TW]], axis=-1)
    elif row_step > 0:
        values = jnp.concatenate([values[..., TW:], values[..., -TW:]], axis=-1)
    if col_step != 0:
        in_row = jnp.arange(values.shape[-1]) % TW
        if col_step < 0:
            shifted = jnp.concatenate([values[..., :1], values[..., :-1]], axis=-1)
            at_edge = in_row == 0
        else:
            shifted = jnp.concatenate([values[..., 1:], values[..., -1:]], axis=-1)
            at_edge = in_row == TW - 1
        values = jnp.where(at_edge, values, shifted)
    return values


def spread_taps(values):
    pieces = []
    for row_step in range(3):
        for col_step in range(3):
            pieces.append(shift_pixels(values, row_step - 1, col_step - 1))
    return jnp.concatenate(pieces, axis=2)


def causal_conv(values, weight, offset):
    columns = spread_taps(values)
    steps_out = values.shape[1] - 2
    summed = jnp.einsum(
        "sfkp,ko->sfop", columns[:, 0:steps_out], weight[0], preferred_element_type=jnp.float32
    )
    for time_lag in (1, 2):
        summed = summed + jnp.einsum(
            "sfkp,ko->sfop",
            columns[:, time_lag : time_lag + steps_out],
            weight[time_lag],
            preferred_element_type=jnp.float32,
        )
    return summed + offset[None, None, :, None]


def per_device(
    latents,
    writer,
    margin_cols,
    in_weight,
    in_bias,
    mid_weight,
    mid_bias,
    skip_weight,
    head_weight,
    head_bias,
):
    home_count = latents.shape[0]
    frame_count = latents.shape[1]
    tile_total = writer.shape[0]
    device = lax.axis_index("tile")
    group_index = lax.axis_index("tm")
    first_group = group_index == 0
    tile_ids = jnp.arange(tile_total, dtype=jnp.int32)
    earlier = (writer[None, :] == writer[:, None]) & (tile_ids[None, :] < tile_ids[:, None])
    slot_rank = jnp.sum(earlier.astype(jnp.int32), axis=1)
    slot_ids = jnp.arange(MAXLOAD, dtype=jnp.int32)
    owned_slot = (writer[:, None] == device) & (slot_rank[:, None] == slot_ids[None, :])
    placing = owned_slot.astype(jnp.bfloat16)
    live_slot = jnp.any(owned_slot, axis=0)
    incoming = lax.all_gather(latents, "tile", axis=0, tiled=True)
    piece_rows = incoming.shape[0]
    chooser = placing
    picked = jnp.einsum(
        "tj,tx->jx", chooser, incoming.reshape(piece_rows, -1), preferred_element_type=jnp.float32
    )
    picked = picked.astype(jnp.bfloat16).reshape(
        MAXLOAD, frame_count, latents.shape[2], latents.shape[3]
    )
    received = from_behind(picked, "tm", 1)
    leading = jnp.where(first_group, jnp.repeat(picked[:, :1], 2, axis=1), received)
    padded_in = jnp.concatenate([leading, picked], axis=1)
    first_out = causal_conv(padded_in, in_weight, in_bias).astype(jnp.bfloat16)
    active = jax.nn.silu(first_out.astype(jnp.float32)).astype(jnp.bfloat16)
    arrived = from_behind(active, "tm", 1)
    leading_act = jnp.where(first_group, jnp.repeat(active[:, :1], 2, axis=1), arrived)
    active = jnp.concatenate([leading_act, active], axis=1)
    middle = causal_conv(active, mid_weight, mid_bias)
    middle = middle + jnp.einsum(
        "sfcp,co->sfop", first_out, skip_weight, preferred_element_type=jnp.float32
    )
    gated_mid = jax.nn.silu(middle).astype(jnp.bfloat16)
    pixels = jnp.einsum("sfcp,co->sfop", gated_mid, head_weight, preferred_element_type=jnp.float32)
    slot_pixels = (pixels + head_bias[None, None, :, None]).astype(jnp.bfloat16)
    written = jnp.where(live_slot[:, None, None, None], slot_pixels, jnp.zeros_like(slot_pixels))
    flat_slots = written.reshape(MAXLOAD, -1)
    chooser = placing
    home_flat = lax.psum_scatter(
        jnp.einsum("tj,jx->tx", chooser, flat_slots, preferred_element_type=jnp.float32).astype(
            jnp.bfloat16
        ),
        "tile",
        scatter_dimension=0,
        tiled=True,
    )
    decoded = home_flat.reshape(home_count, frame_count, 3, -1)
    tile_grid = decoded.reshape(home_count, frame_count, 3, TH, TW)
    rim_cols = tile_grid[..., TW - MARGIN_HI :]
    before_rim = from_behind(rim_cols, "tile", 1)
    prior_rim = jnp.concatenate([before_rim, rim_cols[:-1]], axis=0)
    columns = jnp.arange(TW, dtype=jnp.int32)
    rim_index = jnp.arange(MARGIN_HI, dtype=jnp.int32)
    widths = margin_cols[:, None]
    inside = columns[None, :] < widths
    chooser = (
        rim_index[None, None, :] == MARGIN_HI - widths[:, :, None] + columns[None, :, None]
    ) & inside[:, :, None]
    from_prior = jnp.einsum(
        "tfcry,txy->tfcrx",
        prior_rim,
        chooser.astype(jnp.bfloat16),
        preferred_element_type=jnp.float32,
    )
    fraction = columns[None, :].astype(jnp.float32) / jnp.maximum(widths, 1).astype(jnp.float32)
    weight_new = jnp.where(inside, fraction, 1.0)
    weight_old = jnp.where(inside, 1.0 - fraction, 0.0)
    blended = (
        tile_grid.astype(jnp.float32) * weight_new[:, None, None, None, :]
        + from_prior * weight_old[:, None, None, None, :]
    )
    blended = blended.astype(jnp.bfloat16).reshape(home_count, frame_count, 3, TH * TW)
    return (written, blended)


def solution(mesh):
    return jax.shard_map(
        per_device,
        mesh=mesh,
        in_specs=(P("tile", "tm", None, None), P(), P("tile"), P(), P(), P(), P(), P(), P(), P()),
        out_specs=(P("tile", "tm", None, None), P("tile", "tm", None, None)),
        check_vma=False,
    )
```

profile of v0, /device:TPU:129, one launch (start us, length us, event | category | flops | bytes accessed | tf_op | source)
XLA Modules:
  0.0 267.7 jit_solution(14090642555074421764)
XLA Ops:
  7.2 25.6 %all_gather.3 = bf16[32,2,16,256]{3,2,1,0:T(8,128)(2,1)S(1)} all-gather(bf16[1,2,16,256]{3,2,1,0:T(8,128)(2,1)} %param.10), channel_id=1, replica_groups=mesh['tm'=8,'tile'=32] {'tile'}, dimensions={0}, use_global_device_ids=true | all-gather | bytes 540672 | tf_op jit(solution)/shard_map/all_gather | solution.py:84
  34.9 2.6 collective-permute-start
  37.6 3.3 %collective-permute-done = bf16[3,2,16,256]{3,2,1,0:T(8,128)(2,1)S(1)} collective-permute-done((bf16[3,2,16,256]{3,2,1,0:T(8,128)(2,1)S(1)}, bf16[3,2,16,256]{3,2,1,0:T(8,128)(2,1)S(1)}, u32[]{:S(2)}, u32[]{:S(2)}) %collective-permute-start) | collective-permute-done | bytes 49184 | tf_op jit(solution)/shard_map/ppermute | solution.py:15
  43.8 1.2 fusion.3
  45.0 2.1 collective-permute-start.1
  48.6 34.1 %collective-permute-done.1 = bf16[3,2,512,256]{2,3,1,0:T(8,128)(2,1)S(1)} collective-permute-done((bf16[3,2,512,256]{2,3,1,0:T(8,128)(2,1)S(1)}, bf16[3,2,512,256]{2,3,1,0:T(8,128)(2,1)S(1)}, u32[]{:S(2)}, u32[]{:S(2)}) %collective-permute-start.1) | collective-permute-done | bytes 1572896 | tf_op jit(solution)/shard_map/ppermute | solution.py:15
  84.6 1.1 fusion.15
  85.6 3.0 %fusion.9 = bf16[3,4,4608,256]{2,3,1,0:T(8,128)(2,1)} fusion(bf16[3,4,512,1]{2,3,1,0:T(2,128)(2,1)S(1)} %get-tuple-element.15, bf16[3,4,512,255]{2,3,1,0:T(8,128)(2,1)S(1)} %get-tuple-element.25, pred[256]{0:T(512)(128)(4,1)S(1)} %broadcast_compare_fusion, bf16[3,4,512,240]{2,3,1,0:T(8,128)(2,1)S(1)} %get-tuple-element.19, ...), kind=kLoop, calls=%fused_computation.43 | loop fusion | flops 14155775 | bytes 9437440
  88.7 2.0 fusion.45
  90.7 4.2 %fusion.18 = bf16[3,4,4608,256]{2,3,1,0:T(8,128)(2,1)} fusion(bf16[3,4,4608,256]{2,3,1,0:T(8,128)(2,1)} %fusion.45, bf16[3,4,512,1]{2,3,1,0:T(2,128)(2,1)S(1)} %get-tuple-element.16, bf16[3,4,512,255]{2,3,1,0:T(8,128)(2,1)S(1)} %get-tuple-element.24, pred[256]{0:T(512)(128)(4,1)S(1)} %broadcast_compare_fusion.1, ...), kind=kLoop, calls=%fused_computation.53 | loop fusion | flops 14155776 | bytes 9437440
  94.9 3.0 %fusion.11 = bf16[3,4,4608,256]{2,3,1,0:T(8,128)(2,1)} fusion(bf16[3,4,4608,256]{2,3,1,0:T(8,128)(2,1)} %fusion.18, bf16[3,4,512,1]{2,3,1,0:T(2,128)(2,1)S(1)} %get-tuple-element.15, bf16[3,4,512,255]{2,3,1,0:T(8,128)(2,1)S(1)} %get-tuple-element.23, pred[256]{0:T(512)(128)(4,1)S(1)} %broadcast_compare_fusion, ...), kind=kLoop, calls=%fused_computation.45 | loop fusion | flops 14155776 | bytes 9437440
  97.9 1.9 fusion.46
  99.8 1.2 fusion.13
  101.0 4.1 %fusion.5 = bf16[3,4,4608,256]{2,3,1,0:T(8,128)(2,1)} fusion(bf16[3,4,4608,256]{2,3,1,0:T(8,128)(2,1)} %fusion.46, bf16[3,4,512,1]{2,3,1,0:T(2,128)(2,1)S(1)} %get-tuple-element.17, bf16[3,4,512,255]{2,3,1,0:T(8,128)(2,1)S(1)} %get-tuple-element.22, pred[256]{0:T(512)(128)(4,1)S(1)} %broadcast_compare_fusion.1, ...), kind=kLoop, calls=%fused_computation.39 | loop fusion | flops 14155776 | bytes 9437440
  105.1 3.9 %fusion.19 = bf16[3,4,4608,256]{2,3,1,0:T(8,128)(2,1)} fusion(bf16[3,4,4608,256]{2,3,1,0:T(8,128)(2,1)} %fusion.5, bf16[3,4,512,255]{2,3,1,0:T(8,128)(2,1)S(1)} %get-tuple-element.13, bf16[3,4,512,1]{2,3,1,0:T(2,128)(2,1)S(1)} %get-tuple-element.14, pred[256]{0:T(512)(128)(4,1)S(1)} %broadcast_compare_fusion, ...), kind=kLoop, calls=%fused_computation.55 | loop fusion | flops 14155776 | bytes 9437440
  109.0 2.0 fusion.44
  110.9 5.2 %fusion.7 = bf16[3,4,4608,256]{2,3,1,0:T(8,128)(2,1)} fusion(bf16[3,4,4608,256]{2,3,1,0:T(8,128)(2,1)} %fusion.44, bf16[3,4,512,1]{2,3,1,0:T(2,128)(2,1)S(1)} %get-tuple-element.17, bf16[3,4,512,255]{2,3,1,0:T(8,128)(2,1)S(1)} %get-tuple-element.12, pred[256]{0:T(512)(128)(4,1)S(1)} %broadcast_compare_fusion.1, ...), kind=kLoop, calls=%fused_computation.41 | loop fusion | flops 14155776 | bytes 9437440 | tf_op jit(solution)/shard_map/concatenate | solution.py:40
  116.1 7.3 %fusion.26 = f32[3,2,256,256]{3,2,1,0:T(8,128)S(1)} fusion(bf16[3,4,4608,256]{2,3,1,0:T(8,128)(2,1)} %fusion.7, bf16[3,4608,256]{2,1,0:T(8,128)(2,1)S(1)} %bitcast.128), kind=kOutput, calls=%fused_computation.63 | convolution fusion | flops 3623878656 | bytes 32243712 | tf_op jit(solution)/shard_map/sfkp,ko->sfop/dot_general | solution.py:46
  123.5 8.4 %fusion.24 = f32[3,2,256,256]{3,2,1,0:T(8,128)} fusion(bf16[3,4,4608,256]{2,3,1,0:T(8,128)(2,1)} %fusion.7, bf16[3,4608,256]{2,1,0:T(8,128)(2,1)S(1)} %bitcast.128), kind=kOutput, calls=%fused_computation.61 | convolution fusion | flops 3623878656 | bytes 32243712 | tf_op jit(solution)/shard_map/sfkp,ko->sfop/dot_general | solution.py:50
  131.8 10.6 %fusion.43 = bf16[3,2,3,256]{3,2,1,0:T(4,128)(2,1)S(1)} fusion(f32[3,2,256,256]{3,2,1,0:T(8,128)S(1)} %fusion.34, f32[3,2,256,256]{3,2,1,0:T(8,128)S(1)} %fusion.26, f32[3,2,256,256]{3,2,1,0:T(8,128)} %fusion.24, bf16[3,4,4608,256]{2,3,1,0:T(8,128)(2,1)} %fusion.7, bf16[3,4608,256]{2,1,0:T(8,128)(2,1)} %param.15, f32[256]{0:T(256)S(1)} %copy-done.5, ...), kind=kOutput, calls=%fused_computation.84 | convolution fusion | flops 3629790720 | bytes 35401232 | tf_op jit(solution)/shard_map/sfcp,co->sfop/dot_general | solution.py:106
  144.0 108.4 %all-reduce.3.cloned.1.call-done = bf16[32,1536]{1,0:T(8,128)(2,1)} async-done(((bf16[32,1536]{1,0:T(8,128)(2,1)}), bf16[32,1536]{1,0:T(8,128)(2,1)}) %all-reduce.3.cloned.1.call-update) | async-done | bytes 98320
  252.4 1.4 dynamic-slice_reduce_fusion
  254.1 3.8 %collective-permute-start.2 = (bf16[1,2,3,16,4]{3,4,2,1,0:T(4,128)(2,1)S(1)}, bf16[1,2,3,16,4]{3,4,2,1,0:T(4,128)(2,1)S(1)}, u32[]{:S(2)}, u32[]{:S(2)}) collective-permute-start(bf16[1,2,3,16,4]{3,4,2,1,0:T(4,128)(2,1)S(1)} %copy.42), channel_id=1, source_target_pairs={{0,1},{1,2},{2,3},{3,4},{4,5},{5,6},{6,7},{7,8},{8,9},{9,10},{10,1... | collective-permute-start | bytes 2312 | tf_op jit(solution)/shard_map/ppermute | solution.py:15
  258.5 1.4 convert_reduce_fusion.1
  (71 shorter events, 10.8 us)
Async XLA Ops:
  7.2 40.8 %copy-start = (bf16[512,256]{1,0:T(8,128)(2,1)S(1)}, bf16[512,256]{1,0:T(8,128)(2,1)}, u32[]{:S(2)}) copy-start(bf16[512,256]{1,0:T(8,128)(2,1)} %param.17) | copy-start | bytes 786436
  7.2 245.2 %all-reduce.3.cloned.1.call-start = ((), (), s32[]{:S(2)}) async-start(), calls=%async_computation | async-start | bytes 196608
  32.8 9.7 %copy-start.2 = (bf16[3,144,512]{2,1,0:T(8,128)(2,1)S(1)}, bf16[3,144,512]{2,1,0:T(8,128)(2,1)}, u32[]{:S(2)}) copy-start(bf16[3,144,512]{2,1,0:T(8,128)(2,1)} %param.13) | copy-start | bytes 1327108
  34.9 6.0 %collective-permute-start = (bf16[3,2,16,256]{3,2,1,0:T(8,128)(2,1)S(1)}, bf16[3,2,16,256]{3,2,1,0:T(8,128)(2,1)S(1)}, u32[]{:S(2)}, u32[]{:S(2)}) collective-permute-start(bf16[3,2,16,256]{3,2,1,0:T(8,128)(2,1)S(1)} %bitcast.115), channel_id=1, source_target_pairs={{0,32},{32,64},{64,96},{96,128},{128,160},{160,192},{192,224},{1,3... | collective-permute-start | bytes 147464 | tf_op jit(solution)/shard_map/ppermute | solution.py:15
  42.5 1.3 copy-start.3
  45.0 37.7 %collective-permute-start.1 = (bf16[3,2,512,256]{2,3,1,0:T(8,128)(2,1)S(1)}, bf16[3,2,512,256]{2,3,1,0:T(8,128)(2,1)S(1)}, u32[]{:S(2)}, u32[]{:S(2)}) collective-permute-start(bf16[3,2,512,256]{2,3,1,0:T(8,128)(2,1)S(1)} %get-tuple-element.40), channel_id=1, source_target_pairs={{0,32},{32,64},{64,96},{96,128},{128,160},{160,192},{192,224},{1,3... | collective-permute-start | bytes 4718600 | tf_op jit(solution)/shard_map/ppermute | solution.py:15
  108.9 7.2 %slice-start = ((s8[7077888]{0:T(1024)(128)(4,1)}), s8[4194304]{0:T(1024)(128)(4,1)S(1)}, s32[]{:S(2)}) async-start(s8[7077888]{0:T(1024)(128)(4,1)} %bitcast.127), calls=%async_computation.1 | async-start | bytes 8388608
  110.9 5.2 %slice-start.1 = ((s8[7077888]{0:T(1024)(128)(4,1)}), s8[2883584]{0:T(1024)(128)(4,1)S(1)}, s32[]{:S(2)}) async-start(s8[7077888]{0:T(1024)(128)(4,1)} %bitcast.127), calls=%async_computation.2 | async-start | bytes 5767168
  123.4 8.4 %copy-start.4 = (bf16[256,3]{0,1:T(4,128)(2,1)S(1)}, bf16[256,3]{0,1:T(4,128)(2,1)}, u32[]{:S(2)}) copy-start(bf16[256,3]{0,1:T(4,128)(2,1)} %param.18) | copy-start | bytes 4612
  123.4 8.4 %copy-start.5 = (f32[256]{0:T(256)S(1)}, f32[256]{0:T(256)}, u32[]{:S(2)}) copy-start(f32[256]{0:T(256)} %param.16) | copy-start | bytes 3076
  123.4 8.4 %copy-start.6 = (f32[3]{0:T(128)S(1)}, f32[3]{0:T(128)}, u32[]{:S(2)}) copy-start(f32[3]{0:T(128)} %param.19) | copy-start | bytes 40
  131.8 11.6 %copy-start.7 = (u32[256]{0:T(256)S(1)}, u32[256]{0:T(256)}, u32[]{:S(2)}) copy-start(u32[256]{0:T(256)} %constant.84) | copy-start | bytes 3076
  131.8 129.0 %copy-start.1 = (bf16[512,256]{1,0:T(8,128)(2,1)S(1)}, bf16[512,256]{1,0:T(8,128)(2,1)}, u32[]{:S(2)}) copy-start(bf16[512,256]{1,0:T(8,128)(2,1)} %param.17) | copy-start | bytes 786436
  254.1 5.9 %collective-permute-start.2 = (bf16[1,2,3,16,4]{3,4,2,1,0:T(4,128)(2,1)S(1)}, bf16[1,2,3,16,4]{3,4,2,1,0:T(4,128)(2,1)S(1)}, u32[]{:S(2)}, u32[]{:S(2)}) collective-permute-start(bf16[1,2,3,16,4]{3,4,2,1,0:T(4,128)(2,1)S(1)} %copy.42), channel_id=1, source_target_pairs={{0,1},{1,2},{2,3},{3,4},{4,5},{5,6},{6,7},{7,8},{8,9},{9,10},{10,1... | collective-permute-start | bytes 2312 | tf_op jit(solution)/shard_map/ppermute | solution.py:15
Sparse Core Ops, SparseCore 0:
  143.5 108.8 all-reduce.2
where the time goes:
time: 271 us; the launch traced here: 268 us
  waiting for transfers between devices  146 us (54%)
  other arithmetic  38 us (14%)
  matrix products  30.6 us (11%)
  blocking collectives  25.6 us (9%)
  between operations  15.1 us (6%)
  starting transfers between devices  8.55 us (3%)
  local copies, waits for them, and re-layouts  4.1 us (2%)
    unnamed x2, waiting for transfers between devices  108 us
    ppermute x3, waiting for transfers between devices, from_behind(): return lax.ppermute(block, axis, route)  37.5 us
    all_gather x1, blocking collectives, per_device(): incoming = lax.all_gather(latents, 'tile', axis=0, tiled=True)  25.6 us
    unnamed x17, other arithmetic  24.9 us
    dot_general x1, matrix products, per_device(): jnp.einsum('sfcp,co->sfop', gated_mid, head_weight, preferred_element_typ...  10.6 us
    dot_general x3, matrix products, causal_conv(): jnp.einsum('sfkp,ko->sfop', columns[:, time_lag:time_lag + steps_out], we...  10.2 us
    ppermute x3, starting transfers between devices, from_behind(): return lax.ppermute(block, axis, route)  8.52 us
    dot_general x2, matrix products, causal_conv(): jnp.einsum('sfkp,ko->sfop', columns[:, 0:steps_out], weight[0], preferred...  7.89 us
  transfers between devices with their start and end apart: 4, of which 3 were waited for; matrix products, arithmetic and copies ran while one was open for 1% of the time, Pallas kernels for 0%

commit v1 on v0

v1 whole, which is shorter than its diff:
```python
import jax
import jax.numpy as jnp
from jax import lax
from jax.experimental import pallas as pl
from jax.experimental.pallas import tpu as pltpu
from jax.sharding import PartitionSpec as P

TH = 16
TW = 16
PIX = TH * TW
C_LAT = 16
C_MID = 512
C_OUT = 256
TAPS = 9 * C_LAT
MAXLOAD = 3
MARGIN_LO = 2
MARGIN_HI = 4
MESH = pl.DeviceIdType.MESH
F32 = jnp.float32
BF16 = jnp.bfloat16


def silu(v):
    return 0.5 * v * (1.0 + jnp.tanh(0.5 * v))


def remote(src, dst, send_sem, recv_sem, tm, tile):
    return pltpu.make_async_remote_copy(
        src_ref=src,
        dst_ref=dst,
        send_sem=send_sem,
        recv_sem=recv_sem,
        device_id=(tm, tile),
        device_id_type=MESH,
    )


def spread_columns(cols, lat, first, count):
    lane = lax.broadcasted_iota(jnp.int32, (count * C_LAT, PIX), 1)
    in_row = lane % TW
    x = lat[first : first + count].astype(F32).reshape(count * C_LAT, PIX)
    up = jnp.where(lane < TW, x, pltpu.roll(x, TW, 1))
    down = jnp.where(lane >= PIX - TW, x, pltpu.roll(x, PIX - TW, 1))
    for a, v in enumerate((up, x, down)):
        left = jnp.where(in_row == 0, v, pltpu.roll(v, 1, 1))
        right = jnp.where(in_row == TW - 1, v, pltpu.roll(v, PIX - 1, 1))
        for e, s in enumerate((left, v, right)):
            s = s.astype(BF16)
            for k in range(count):
                at = (first + k) * TAPS + (3 * a + e) * C_LAT
                cols[at : at + C_LAT, :] = s[k * C_LAT : (k + 1) * C_LAT]


def shift_rows(z, in_row, step):
    if step < 0:
        return jnp.where(in_row == 0, z, pltpu.roll(z, 1, 0))
    return jnp.where(in_row == TW - 1, z, pltpu.roll(z, PIX - 1, 0))


def decode_kernel(
    tiles,
    groups,
    lat_in,
    writer_in,
    margin_in,
    in_w_in,
    in_b_in,
    mid_w_in,
    mid_b_in,
    skip_w_in,
    head_w_in,
    head_b_in,
    written_out,
    blended_out,
    lat,
    cols,
    w_in,
    b_in,
    w_mid,
    b_mid,
    w_skip,
    w_head,
    u,
    v,
    first_out,
    acc,
    gated,
    gather,
    written,
    blended,
    s_writer,
    s_margin,
    s_head_b,
    halo_send,
    halo_recv,
    all_send,
    all_recv,
    load_sem,
    chunk_sem,
    out_sem,
):
    tm = lax.axis_index("tm")
    tile = lax.axis_index("tile")

    barrier = pltpu.get_barrier_semaphore()
    for d in (1, 2):

        @pl.when(tm >= d)
        def _():
            pl.semaphore_signal(barrier, inc=1, device_id=(tm - d, tile), device_id_type=MESH)

    own = pltpu.make_async_copy(lat_in.at[0], lat.at[4:6], load_sem.at[0])
    own.start()
    loads = []
    for k, (src, dst) in enumerate(
        (
            (in_w_in, w_in),
            (in_b_in, b_in),
            (head_w_in, w_head),
            (mid_b_in, b_mid),
            (writer_in, s_writer),
            (margin_in, s_margin),
            (head_b_in, s_head_b),
            (skip_w_in, w_skip),
        )
    ):
        copy = pltpu.make_async_copy(src, dst, load_sem.at[k + 1])
        copy.start()
        loads.append(copy)
    chunks = []
    for k in range(9):
        rows = slice(k * C_MID, (k + 1) * C_MID)
        copy = pltpu.make_async_copy(mid_w_in.at[:, rows], w_mid.at[:, rows], chunk_sem.at[k])
        copy.start()
        chunks.append(copy)
    for i in range(1, tiles):
        pl.semaphore_signal(
            barrier, inc=1, device_id=(tm, lax.rem(tile + i, tiles)), device_id_type=MESH
        )
    expected = (
        tiles - 1 + (tm < groups - 1).astype(jnp.int32) + (tm < groups - 2).astype(jnp.int32)
    )
    pl.semaphore_wait(barrier, expected)

    def halo(d):
        return remote(
            lat_in.at[0],
            lat.at[4 - 2 * d : 6 - 2 * d],
            halo_send.at[d - 1],
            halo_recv.at[d - 1],
            tm + d if d > 0 else tm,
            tile,
        )

    for d in (1, 2):

        @pl.when(tm < groups - d)
        def _():
            halo(d).start()

    own.wait()
    spread_columns(cols, lat, 4, 2)

    for k in range(9):
        chunks[k].wait()

        @pl.loop(0, C_MID // 64)
        def _(s):
            rows = pl.ds(pl.multiple_of(k * C_MID + s * 64, 64), 64)
            even = w_mid[0, rows, :].astype(F32) + w_mid[2, rows, :].astype(F32)
            odd = w_mid[1, rows, :].astype(F32)
            u[0, rows, :] = (even + odd).astype(BF16)
            u[1, rows, :] = (even - odd).astype(BF16)

    for copy in loads:
        copy.wait()

    for d in (1, 2):

        @pl.when(tm >= d)
        def _():
            halo(d).wait_recv()

    @pl.when(tm == 0)
    def _():
        for g in range(4):
            lat[g] = lat[4]

    @pl.when(tm == 1)
    def _():
        for g in range(2):
            lat[g] = lat[2]

    spread_columns(cols, lat, 0, 4)

    weight = w_in[...].reshape(3 * TAPS, C_MID)
    acts = []
    for j in range(4):
        out = lax.dot_general(
            cols[j * TAPS : (j + 3) * TAPS, :],
            weight,
            (((0,), (0,)), ((), ())),
            preferred_element_type=F32,
        )
        out = (out + b_in[...]).astype(BF16)
        if j >= 2:
            first_out[j - 2] = out
        acts.append(silu(out.astype(F32)))
        if j == 2:
            mixed = (
                (0, acts[0] - acts[2]),
                (1, 0.5 * (acts[1] + acts[2])),
                (2, 0.5 * (acts[2] - acts[1])),
            )
        elif j == 3:
            mixed = ((3, acts[1] - acts[3]),)
        else:
            mixed = ()
        for i, m in mixed:
            m = m.astype(BF16)
            v[i, TW : TW + PIX, :] = m
            v[i, 0:TW, :] = m[0:TW]
            v[i, TW + PIX : 2 * TW + PIX, :] = m[PIX - TW : PIX]

    in_row = lax.broadcasted_iota(jnp.int32, (PIX, C_OUT), 0) % TW

    def product(i, e):
        frames, weights = [], []
        for r in range(3):
            rows = slice((3 * r + e) * C_MID, (3 * r + e + 1) * C_MID)
            frames.append(v[i, TW * r : TW * r + PIX, :])
            if i in (0, 3):
                weights.append(w_mid[0 if i == 0 else 2, rows, :])
            else:
                weights.append(u[i - 1, rows, :])
        return jnp.dot(
            jnp.concatenate(frames, axis=1),
            jnp.concatenate(weights, axis=0),
            preferred_element_type=F32,
        )

    def finish(f, sums):
        total = sums[1] + shift_rows(sums[0], in_row, -1) + shift_rows(sums[2], in_row, 1)
        total = total + jnp.dot(first_out[f], w_skip[...], preferred_element_type=F32) + b_mid[...]
        gated[:, f * C_OUT : (f + 1) * C_OUT] = silu(total).astype(BF16)

    for e in range(3):
        p1 = product(1, e)
        acc[0, e] = p1
        acc[1, e] = p1
    for e in range(3):
        p2 = product(2, e)
        acc[0, e] += p2
        acc[1, e] -= p2
    finish(0, [acc[0, e] + product(0, e) for e in range(3)])
    finish(1, [acc[1, e] - product(3, e) for e in range(3)])

    row = lax.broadcasted_iota(jnp.int32, (8, C_OUT), 0)
    head = w_head[...].astype(F32)
    by_color = jnp.where(
        row // 2 == 0,
        head[0:1],
        jnp.where(row // 2 == 1, head[1:2], jnp.where(row // 2 == 2, head[2:3], 0.0)),
    )
    head2 = jnp.concatenate(
        [jnp.where(row % 2 == 0, by_color, 0.0), jnp.where(row % 2 == 1, by_color, 0.0)], axis=1
    ).astype(BF16)
    pixels = lax.dot_general(
        head2, gated[...], (((1,), (1,)), ((), ())), preferred_element_type=F32
    )
    pixels = pixels + jnp.where(
        row // 2 == 0, s_head_b[0], jnp.where(row // 2 == 1, s_head_b[1], s_head_b[2])
    )
    gather[tile] = jnp.concatenate([pixels[:, :128], pixels[:, 128:]], axis=0).astype(BF16)

    for i in range(1, tiles):
        to = lax.rem(tile + i, tiles)
        remote(gather.at[tile], gather.at[tile], all_send, all_recv, tm, to).start()
    everyone = remote(
        gather.at[0 : tiles - 1],
        gather.at[0 : tiles - 1],
        all_send,
        all_recv,
        tm,
        lax.rem(tile + 1, tiles),
    )

    found = jnp.int32(0)
    which = [jnp.int32(0)] * MAXLOAD
    taken = [jnp.int32(0)] * MAXLOAD
    for t in range(tiles):
        mine = s_writer[t] == tile
        for j in range(MAXLOAD):
            hit = jnp.logical_and(mine, found == j)
            which[j] = jnp.where(hit, t, which[j])
            taken[j] = jnp.where(hit, 1, taken[j])
        found = found + mine.astype(jnp.int32)

    everyone.wait_recv()

    def tile_pixels(t):
        block = gather[t].astype(F32)
        return jnp.concatenate([block[0:8], block[8:16]], axis=1)

    for j in range(MAXLOAD):
        live = jnp.full((8, PIX), taken[j], jnp.int32) > 0
        block = jnp.where(live, tile_pixels(which[j]), 0.0).astype(BF16)
        for c in range(3):
            written[j, c] = block[2 * c : 2 * c + 2]
    margin = s_margin[0]
    width = jnp.full((8, PIX), margin, jnp.int32)
    column = lax.broadcasted_iota(jnp.int32, (8, PIX), 1) % TW
    current = tile_pixels(tile)
    before = tile_pixels(jnp.maximum(tile - 1, 0))
    prior = pltpu.roll(before, PIX - TW + MARGIN_LO, 1)
    for m in range(MARGIN_LO + 1, MARGIN_HI + 1):
        prior = jnp.where(width == m, pltpu.roll(before, PIX - TW + m, 1), prior)
    fraction = column.astype(F32) / jnp.maximum(width, 1).astype(F32)
    mix = jnp.where(column < width, (1.0 - fraction) * prior + fraction * current, current)
    mix = mix.astype(BF16)
    for c in range(3):
        blended[0, c] = mix[2 * c : 2 * c + 2]
    outs = [
        pltpu.make_async_copy(written, written_out, out_sem.at[0]),
        pltpu.make_async_copy(blended, blended_out, out_sem.at[1]),
    ]
    for copy in outs:
        copy.start()
    everyone.wait_send()
    for d in (1, 2):

        @pl.when(tm < groups - d)
        def _():
            halo(d).wait_send()

    for copy in outs:
        copy.wait()


def copy_kernel(written_in, blended_in, written_out, blended_out, sem):
    copies = [
        pltpu.make_async_copy(written_in, written_out, sem.at[0]),
        pltpu.make_async_copy(blended_in, blended_out, sem.at[1]),
    ]
    for copy in copies:
        copy.start()
    for copy in copies:
        copy.wait()


def per_device(
    latents,
    writer,
    margin_cols,
    in_weight,
    in_bias,
    mid_weight,
    mid_bias,
    skip_weight,
    head_weight,
    head_bias,
):
    tiles = lax.axis_size("tile")
    groups = lax.axis_size("tm")
    frames = latents.shape[1]
    shapes = (
        jax.ShapeDtypeStruct((MAXLOAD, 3, frames, PIX), BF16),
        jax.ShapeDtypeStruct((1, 3, frames, PIX), BF16),
    )
    anywhere = pl.BlockSpec(memory_space=pl.ANY)

    def body(*refs):
        decode_kernel(tiles, groups, *refs)

    written, blended = pl.pallas_call(
        body,
        out_shape=shapes,
        in_specs=[anywhere] * 10,
        out_specs=(anywhere,) * 2,
        scratch_shapes=[
            pltpu.VMEM((6, C_LAT, PIX), BF16),
            pltpu.VMEM((6 * TAPS, PIX), BF16),
            pltpu.VMEM((3, TAPS, C_MID), BF16),
            pltpu.VMEM((1, C_MID), F32),
            pltpu.VMEM((3, 9 * C_MID, C_OUT), BF16),
            pltpu.VMEM((1, C_OUT), F32),
            pltpu.VMEM((C_MID, C_OUT), BF16),
            pltpu.VMEM((3, C_OUT), BF16),
            pltpu.VMEM((2, 9 * C_MID, C_OUT), BF16),
            pltpu.VMEM((4, PIX + 2 * TW, C_MID), BF16),
            pltpu.VMEM((2, PIX, C_MID), BF16),
            pltpu.VMEM((2, 3, PIX, C_OUT), F32),
            pltpu.VMEM((PIX, 2 * C_OUT), BF16),
            pltpu.VMEM((tiles, 16, 128), BF16),
            pltpu.VMEM((MAXLOAD, 3, frames, PIX), BF16),
            pltpu.VMEM((1, 3, frames, PIX), BF16),
            pltpu.SMEM((tiles,), jnp.int32),
            pltpu.SMEM((1,), jnp.int32),
            pltpu.SMEM((3,), F32),
            pltpu.SemaphoreType.DMA((2,)),
            pltpu.SemaphoreType.DMA((2,)),
            pltpu.SemaphoreType.DMA,
            pltpu.SemaphoreType.DMA,
            pltpu.SemaphoreType.DMA((9,)),
            pltpu.SemaphoreType.DMA((9,)),
            pltpu.SemaphoreType.DMA((2,)),
        ],
        compiler_params=pltpu.CompilerParams(
            collective_id=0, has_side_effects=True, vmem_limit_bytes=60 * 2**20
        ),
        name="decode",
    )(
        latents,
        writer,
        margin_cols,
        in_weight,
        in_bias.reshape(1, -1),
        mid_weight,
        mid_bias.reshape(1, -1),
        skip_weight,
        head_weight.T,
        head_bias,
    )
    written, blended = pl.pallas_call(
        copy_kernel,
        out_shape=shapes,
        in_specs=[anywhere] * 2,
        out_specs=(anywhere,) * 2,
        scratch_shapes=[pltpu.SemaphoreType.DMA((2,))],
        name="hand_out",
    )(written, blended)
    return written.transpose(0, 2, 1, 3), blended.transpose(0, 2, 1, 3)


def solution(mesh):
    return jax.shard_map(
        per_device,
        mesh=mesh,
        in_specs=(P("tile", "tm", None, None), P(), P("tile"), P(), P(), P(), P(), P(), P(), P()),
        out_specs=(P("tile", "tm", None, None), P("tile", "tm", None, None)),
        check_vma=False,
    )
```

time: 271 us -> 22.3 us (0.08); the launches traced: 268 us -> 22 us
  waiting for transfers between devices: 146 us -> 0 us
  other arithmetic: 38 us -> 0 us
  matrix products: 30.6 us -> 0 us
  blocking collectives: 25.6 us -> 0 us
  Pallas kernels: 0 us -> 20.7 us
  between operations: 15.1 us -> 1.29 us
  starting transfers between devices: 8.55 us -> 0 us
  local copies, waits for them, and re-layouts: 4.1 us -> 0 us
    unnamed x2 -> x0, waiting for transfers between devices: 108 us -> none
    ppermute x3 -> x0, waiting for transfers between devices: 37.5 us -> none  [from_behind(): return lax.ppermute(block, axis, route)]
    dot_general x10 -> x0, matrix products: 30.6 us -> none  [the longest x1 10.6 us: per_device(): jnp.einsum('sfcp,co->sfop', gated_mid, head_weight, preferred_element_typ...]
    all_gather x1 -> x0, blocking collectives: 25.6 us -> none  [per_device(): incoming = lax.all_gather(latents, 'tile', axis=0, tiled=True)]
    unnamed x17 -> x0, other arithmetic: 24.9 us -> none
    pallas_call x0 -> x2, Pallas kernels: none -> 20.7 us  [the longest x1 19.2 us: per_device(): pl.pallas_call(body, out_shape=shapes, in_specs=[anywhere] * 10, out_spec...]
    concatenate x13 -> x0, other arithmetic: 9.8 us -> none  [the longest x2 5.31 us: spread_taps(): return jnp.concatenate(pieces, axis=2)]
    ppermute x3 -> x0, starting transfers between devices: 8.52 us -> none  [from_behind(): return lax.ppermute(block, axis, route)]
  transfers between devices with their start and end apart: 4 -> 0, of which waited for: 3 -> 0; matrix products, arithmetic and copies ran while one was open for 1% -> 0% of each run, Pallas kernels for 0% -> 0%
where the time goes in v1:
time: 22.3 us; the launch traced here: 22 us
  Pallas kernels  20.7 us (93%)
  between operations  1.29 us (6%)
    pallas_call x1, Pallas kernels, per_device(): pl.pallas_call(body, out_shape=shapes, in_specs=[anywhere] * 10, out_spec...  19.2 us
    pallas_call x1, Pallas kernels, per_device(): pl.pallas_call(copy_kernel, out_shape=shapes, in_specs=[anywhere] * 2, ou...  1.49 us

profile of v1, /device:TPU:129, one launch (start us, length us, event | category | flops | bytes accessed | tf_op | source)
XLA Modules:
  0.0 22.0 jit_solution(14868336275146744129)
XLA Ops:
  1.3 19.2 %decode.1 = (bf16[3,3,2,256]{3,2,1,0:T(2,128)(2,1)}, bf16[1,3,2,256]{3,2,1,0:T(2,128)(2,1)}) custom-call(bf16[1,2,16,256]{3,2,1,0:T(8,128)(2,1)} %refs_0_.1, s32[32]{0:T(128)} %refs_1_.1, s32[1]{0:T(128)S(6)} %copy.12.refs_2_, bf16[3,144,512]{2,1,0:T(8,128)(2,1)} %refs_3_.1, f32[1,512]{1,0:T(1,128)} %bitcast.5, bf16[3,4608,256]{2,1,0:T(8,128)(2,1)} %refs_5_.1, ...), custom_call_target="tpu_custom_call" | custom-call | tf_op jit(solution)/shard_map/decode/pallas_call | solution.py:375
  20.5 1.5 %hand_out.1 = (bf16[3,3,2,256]{3,2,1,0:T(2,128)(2,1)}, bf16[1,3,2,256]{3,2,1,0:T(2,128)(2,1)}) custom-call(bf16[3,3,2,256]{3,2,1,0:T(2,128)(2,1)} %get-tuple-element.6.written_in, bf16[1,3,2,256]{3,2,1,0:T(2,128)(2,1)} %get-tuple-element.7.blended_in), custom_call_target="tpu_custom_call" | custom-call | tf_op jit(solution)/shard_map/hand_out/pallas_call | solution.py:424

commit v2 on v1

--- a/solution.py
+++ b/solution.py
@@ -15,7 +15,20 @@
 MAXLOAD = 3
 MARGIN_LO = 2
 MARGIN_HI = 4
+SIDE = 4
+CORES = 2
 MESH = pl.DeviceIdType.MESH
+RELAYED = 3
+FAR_FIRST = sorted(
+    (
+        (dx, dy, dc)
+        for dx in range(SIDE)
+        for dy in range(SIDE)
+        for dc in range(CORES)
+        if dx or dy or dc
+    ),
+    key=lambda p: -min(p[0], SIDE - p[0]) - min(p[1], SIDE - p[1]),
+)
 F32 = jnp.float32
 BF16 = jnp.bfloat16
 
@@ -70,8 +83,8 @@
     skip_w_in,
     head_w_in,
     head_b_in,
-    written_out,
-    blended_out,
+    written,
+    blended,
     lat,
     cols,
     w_in,
@@ -86,8 +99,6 @@
     acc,
     gated,
     gather,
-    written,
-    blended,
     s_writer,
     s_margin,
     s_head_b,
@@ -97,20 +108,60 @@
     all_recv,
     load_sem,
     chunk_sem,
-    out_sem,
+    hop,
+    after,
 ):
     tm = lax.axis_index("tm")
     tile = lax.axis_index("tile")
 
+    core = lax.rem(tile, CORES)
+    y = lax.rem(tile // CORES, SIDE)
+    x = tile // (CORES * SIDE)
+
+    def at(x, y, core):
+        return (lax.rem(x, SIDE) * SIDE + lax.rem(y, SIDE)) * CORES + lax.rem(core, CORES)
+
+    beside_core = (at(x, y, core + 1),)
+    beside_x = (at(x + 1, y, core), at(x + SIDE - 1, y, core))
+    beside_y = (at(x, y + 1, core), at(x, y + SIDE - 1, core))
+
+    def tell(semaphore, peers):
+        for peer in peers:
+            pl.semaphore_signal(semaphore, inc=1, device_id=(tm, peer), device_id_type=MESH)
+
     barrier = pltpu.get_barrier_semaphore()
-    for d in (1, 2):
-
-        @pl.when(tm >= d)
-        def _():
-            pl.semaphore_signal(barrier, inc=1, device_id=(tm - d, tile), device_id_type=MESH)
+    relayed = min(RELAYED, groups - 2)
+
+    @pl.when(tm >= 1)
+    def _():
+        pl.semaphore_signal(barrier, inc=1, device_id=(tm - 1, tile), device_id_type=MESH)
+
+    @pl.when(tm >= relayed + 2)
+    def _():
+        pl.semaphore_signal(barrier, inc=1, device_id=(tm - 2, tile), device_id_type=MESH)
+
+    @pl.when(tm < relayed)
+    def _():
+        pl.semaphore_signal(barrier, inc=1, device_id=(tm + 1, tile), device_id_type=MESH)
+
+    tell(barrier, beside_core + beside_x + beside_y)
 
     own = pltpu.make_async_copy(lat_in.at[0], lat.at[4:6], load_sem.at[0])
     own.start()
+    chunks = []
+
+    def load_chunk(k):
+        rows = slice(k * C_MID, (k + 1) * C_MID)
+        chunk = []
+        for lag in range(3):
+            copy = pltpu.make_async_copy(
+                mid_w_in.at[lag, rows], w_mid.at[lag, rows], chunk_sem.at[3 * k + lag]
+            )
+            copy.start()
+            chunk.append(copy)
+        chunks.append(chunk)
+
+    load_chunk(0)
     loads = []
     for k, (src, dst) in enumerate(
         (
@@ -127,20 +178,8 @@
         copy = pltpu.make_async_copy(src, dst, load_sem.at[k + 1])
         copy.start()
         loads.append(copy)
-    chunks = []
-    for k in range(9):
-        rows = slice(k * C_MID, (k + 1) * C_MID)
-        copy = pltpu.make_async_copy(mid_w_in.at[:, rows], w_mid.at[:, rows], chunk_sem.at[k])
-        copy.start()
-        chunks.append(copy)
-    for i in range(1, tiles):
-        pl.semaphore_signal(
-            barrier, inc=1, device_id=(tm, lax.rem(tile + i, tiles)), device_id_type=MESH
-        )
-    expected = (
-        tiles - 1 + (tm < groups - 1).astype(jnp.int32) + (tm < groups - 2).astype(jnp.int32)
-    )
-    pl.semaphore_wait(barrier, expected)
+    for k in range(1, 9):
+        load_chunk(k)
 
     def halo(d):
         return remote(
@@ -148,21 +187,13 @@
             lat.at[4 - 2 * d : 6 - 2 * d],
             halo_send.at[d - 1],
             halo_recv.at[d - 1],
-            tm + d if d > 0 else tm,
+            lax.rem(tm + d, groups),
             tile,
         )
 
-    for d in (1, 2):
-
-        @pl.when(tm < groups - d)
-        def _():
-            halo(d).start()
-
-    own.wait()
-    spread_columns(cols, lat, 4, 2)
-
-    for k in range(9):
-        chunks[k].wait()
+    def mix_weights(k):
+        for copy in chunks[k]:
+            copy.wait()
 
         @pl.loop(0, C_MID // 64)
         def _(s):
@@ -172,30 +203,50 @@
             u[0, rows, :] = (even + odd).astype(BF16)
             u[1, rows, :] = (even - odd).astype(BF16)
 
+    own.wait()
+    spread_columns(cols, lat, 4, 2)
+    for k in range(2):
+        mix_weights(k)
+
+    expected = (
+        5
+        + (tm < groups - 1).astype(jnp.int32)
+        + jnp.logical_and(tm >= relayed, tm < groups - 2).astype(jnp.int32)
+        + jnp.logical_and(tm >= 1, tm <= relayed).astype(jnp.int32)
+    )
+    pl.semaphore_wait(barrier, expected)
+
+    @pl.when(tm < groups - 1)
+    def _():
+        halo(1).start()
+
+    @pl.when(jnp.logical_and(tm >= relayed, tm < groups - 2))
+    def _():
+        halo(2).start()
+
+    @pl.when(jnp.logical_and(tm >= 1, tm <= relayed))
+    def _():
+        pl.semaphore_signal(after, inc=1, device_id=(tm - 1, tile), device_id_type=MESH)
+
+    tell(hop.at[0], beside_core)
+    for k in range(2, 7):
+        mix_weights(k)
+    pl.semaphore_wait(hop.at[0], 1)
+    tell(hop.at[1], beside_x)
+
+    for k in range(7, 9):
+        mix_weights(k)
     for copy in loads:
         copy.wait()
 
-    for d in (1, 2):
-
-        @pl.when(tm >= d)
-        def _():
-            halo(d).wait_recv()
-
-    @pl.when(tm == 0)
-    def _():
-        for g in range(4):
-            lat[g] = lat[4]
-
-    @pl.when(tm == 1)
-    def _():
-        for g in range(2):
-            lat[g] = lat[2]
-
-    spread_columns(cols, lat, 0, 4)
+    @pl.when(tm < relayed)
+    def _():
+        pl.semaphore_wait(after, 1)
+        halo(2).start()
 
     weight = w_in[...].reshape(3 * TAPS, C_MID)
-    acts = []
-    for j in range(4):
+
+    def features(j):
         out = lax.dot_general(
             cols[j * TAPS : (j + 3) * TAPS, :],
             weight,
@@ -205,22 +256,48 @@
         out = (out + b_in[...]).astype(BF16)
         if j >= 2:
             first_out[j - 2] = out
-        acts.append(silu(out.astype(F32)))
-        if j == 2:
-            mixed = (
-                (0, acts[0] - acts[2]),
-                (1, 0.5 * (acts[1] + acts[2])),
-                (2, 0.5 * (acts[2] - acts[1])),
-            )
-        elif j == 3:
-            mixed = ((3, acts[1] - acts[3]),)
-        else:
-            mixed = ()
-        for i, m in mixed:
-            m = m.astype(BF16)
-            v[i, TW : TW + PIX, :] = m
-            v[i, 0:TW, :] = m[0:TW]
-            v[i, TW + PIX : 2 * TW + PIX, :] = m[PIX - TW : PIX]
+        return silu(out.astype(F32))
+
+    def keep(i, m):
+        m = m.astype(BF16)
+        v[i, TW : TW + PIX, :] = m
+        v[i, 0:TW, :] = m[0:TW]
+        v[i, TW + PIX : 2 * TW + PIX, :] = m[PIX - TW : PIX]
+
+    @pl.when(tm >= 1)
+    def _():
+        halo(1).wait_recv()
+
+    pl.semaphore_wait(hop.at[1], 2)
+    tell(hop.at[2], beside_x)
+
+    @pl.when(tm == 0)
+    def _():
+        for g in range(4):
+            lat[g] = lat[4]
+
+    spread_columns(cols, lat, 2, 2)
+    act2 = features(2)
+    act3 = features(3)
+
+    @pl.when(tm >= 2)
+    def _():
+        halo(2).wait_recv()
+
+    pl.semaphore_wait(hop.at[2], 2)
+    tell(hop.at[3], beside_y)
+
+    @pl.when(tm == 1)
+    def _():
+        for g in range(2):
+            lat[g] = lat[2]
+
+    spread_columns(cols, lat, 0, 2)
+    act1 = features(1)
+    keep(1, 0.5 * (act1 + act2))
+    keep(2, 0.5 * (act2 - act1))
+    keep(3, act1 - act3)
+    keep(0, features(0) - act2)
 
     in_row = lax.broadcasted_iota(jnp.int32, (PIX, C_OUT), 0) % TW
 
@@ -273,8 +350,9 @@
     )
     gather[tile] = jnp.concatenate([pixels[:, :128], pixels[:, 128:]], axis=0).astype(BF16)
 
-    for i in range(1, tiles):
-        to = lax.rem(tile + i, tiles)
+    pl.semaphore_wait(hop.at[3], 2)
+    for dx, dy, dc in FAR_FIRST:
+        to = at(x + dx, y + dy, core + dc)
         remote(gather.at[tile], gather.at[tile], all_send, all_recv, tm, to).start()
     everyone = remote(
         gather.at[0 : tiles - 1],
@@ -307,8 +385,7 @@
         block = jnp.where(live, tile_pixels(which[j]), 0.0).astype(BF16)
         for c in range(3):
             written[j, c] = block[2 * c : 2 * c + 2]
-    margin = s_margin[0]
-    width = jnp.full((8, PIX), margin, jnp.int32)
+    width = jnp.full((8, PIX), s_margin[0], jnp.int32)
     column = lax.broadcasted_iota(jnp.int32, (8, PIX), 1) % TW
     current = tile_pixels(tile)
     before = tile_pixels(jnp.maximum(tile - 1, 0))
@@ -320,21 +397,12 @@
     mix = mix.astype(BF16)
     for c in range(3):
         blended[0, c] = mix[2 * c : 2 * c + 2]
-    outs = [
-        pltpu.make_async_copy(written, written_out, out_sem.at[0]),
-        pltpu.make_async_copy(blended, blended_out, out_sem.at[1]),
-    ]
-    for copy in outs:
-        copy.start()
     everyone.wait_send()
     for d in (1, 2):
 
         @pl.when(tm < groups - d)
         def _():
             halo(d).wait_send()
-
-    for copy in outs:
-        copy.wait()
 
 
 def copy_kernel(written_in, blended_in, written_out, blended_out, sem):
@@ -374,9 +442,9 @@
 
     written, blended = pl.pallas_call(
         body,
-        out_shape=shapes,
+        out_shape=tuple(pltpu.VMEM(s.shape, s.dtype) for s in shapes),
         in_specs=[anywhere] * 10,
-        out_specs=(anywhere,) * 2,
+        out_specs=(pl.BlockSpec(memory_space=pltpu.VMEM),) * 2,
         scratch_shapes=[
             pltpu.VMEM((6, C_LAT, PIX), BF16),
             pltpu.VMEM((6 * TAPS, PIX), BF16),
@@ -392,8 +460,6 @@
             pltpu.VMEM((2, 3, PIX, C_OUT), F32),
             pltpu.VMEM((PIX, 2 * C_OUT), BF16),
             pltpu.VMEM((tiles, 16, 128), BF16),
-            pltpu.VMEM((MAXLOAD, 3, frames, PIX), BF16),
-            pltpu.VMEM((1, 3, frames, PIX), BF16),
             pltpu.SMEM((tiles,), jnp.int32),
             pltpu.SMEM((1,), jnp.int32),
             pltpu.SMEM((3,), F32),
@@ -402,24 +468,30 @@
             pltpu.SemaphoreType.DMA,
             pltpu.SemaphoreType.DMA,
             pltpu.SemaphoreType.DMA((9,)),
-            pltpu.SemaphoreType.DMA((9,)),
-            pltpu.SemaphoreType.DMA((2,)),
+            pltpu.SemaphoreType.DMA((27,)),
+            pltpu.SemaphoreType.REGULAR((4,)),
+            pltpu.SemaphoreType.REGULAR,
         ],
         compiler_params=pltpu.CompilerParams(
             collective_id=0, has_side_effects=True, vmem_limit_bytes=60 * 2**20
         ),
         name="decode",
     )(
-        latents,
-        writer,
-        margin_cols,
-        in_weight,
-        in_bias.reshape(1, -1),
-        mid_weight,
-        mid_bias.reshape(1, -1),
-        skip_weight,
-        head_weight.T,
-        head_bias,
+        *(
+            a if a is margin_cols else pltpu.with_memory_space_constraint(a, pltpu.HBM)
+            for a in (
+                latents,
+                writer,
+                margin_cols,
+                in_weight,
+                in_bias.reshape(1, -1),
+                mid_weight,
+                mid_bias.reshape(1, -1),
+                skip_weight,
+                head_weight.T,
+                head_bias,
+            )
+        )
     )
     written, blended = pl.pallas_call(
         copy_kernel,
@@ -428,7 +500,10 @@
         out_specs=(anywhere,) * 2,
         scratch_shapes=[pltpu.SemaphoreType.DMA((2,))],
         name="hand_out",
-    )(written, blended)
+    )(
+        pltpu.with_memory_space_constraint(written, pltpu.VMEM),
+        pltpu.with_memory_space_constraint(blended, pltpu.VMEM),
+    )
     return written.transpose(0, 2, 1, 3), blended.transpose(0, 2, 1, 3)
 
 

time: 22.3 us -> 21.1 us (0.946)
  Pallas kernels: 20.7 us -> 19.5 us
    pallas_call x1, Pallas kernels: 1.49 us -> 0.62 us  [per_device(): pl.pallas_call(copy_kernel, out_shape=shapes, in_specs=[anywhere] * 2, ou...]
    pallas_call x1, Pallas kernels: 19.2 us -> 18.8 us  [per_device(): pl.pallas_call(body, out_shape=tuple((pltpu.VMEM(s.shape, s.dtype) for s...]
where the time goes in v2:
time: 21.1 us; the launch traced here: 20.8 us
  Pallas kernels  19.5 us (92%)
  between operations  1.29 us (6%)
    pallas_call x1, Pallas kernels, per_device(): pl.pallas_call(body, out_shape=tuple((pltpu.VMEM(s.shape, s.dtype) for s...  18.8 us
    pallas_call x1, Pallas kernels, per_device(): pl.pallas_call(copy_kernel, out_shape=shapes, in_specs=[anywhere] * 2, ou...  0.62 us

profile of v2, /device:TPU:129, one launch (start us, length us, event | category | flops | bytes accessed | tf_op | source)
XLA Modules:
  0.0 20.8 jit_solution(923451580126985825)
XLA Ops:
  1.3 18.8 %decode.1 = (bf16[3,3,2,256]{3,2,1,0:T(2,128)(2,1)S(1)}, bf16[1,3,2,256]{3,2,1,0:T(2,128)(2,1)S(1)}) custom-call(bf16[1,2,16,256]{3,2,1,0:T(8,128)(2,1)} %refs_0_.1, s32[32]{0:T(128)} %refs_1_.1, s32[1]{0:T(128)S(6)} %copy.12.refs_2_, bf16[3,144,512]{2,1,0:T(8,128)(2,1)} %refs_3_.1, f32[1,512]{1,0:T(1,128)} %bitcast.5, bf16[3,4608,256]{2,1,0:T(8,128)(2,1)} %refs_5_.1, ...), custom_call_target="tpu_custom_call" | custom-call | tf_op jit(solution)/shard_map/decode/pallas_call | solution.py:443
  20.1 0.6 %hand_out.1 = (bf16[3,3,2,256]{3,2,1,0:T(2,128)(2,1)}, bf16[1,3,2,256]{3,2,1,0:T(2,128)(2,1)}) custom-call(bf16[3,3,2,256]{3,2,1,0:T(2,128)(2,1)S(1)} %get-tuple-element.6.written_in, bf16[1,3,2,256]{3,2,1,0:T(2,128)(2,1)S(1)} %get-tuple-element.7.blended_in), custom_call_target="tpu_custom_call" | custom-call | tf_op jit(solution)/shard_map/hand_out/pallas_call | solution.py:496

commit v3 on v2

--- a/solution.py
+++ b/solution.py
@@ -18,7 +18,7 @@
 SIDE = 4
 CORES = 2
 MESH = pl.DeviceIdType.MESH
-RELAYED = 3
+RELAYED = 2
 FAR_FIRST = sorted(
     (
         (dx, dy, dc)
@@ -121,9 +121,10 @@
     def at(x, y, core):
         return (lax.rem(x, SIDE) * SIDE + lax.rem(y, SIDE)) * CORES + lax.rem(core, CORES)
 
-    beside_core = (at(x, y, core + 1),)
-    beside_x = (at(x + 1, y, core), at(x + SIDE - 1, y, core))
-    beside_y = (at(x, y + 1, core), at(x, y + SIDE - 1, core))
+    row = tuple(
+        at(x + dx, y, core + dc) for dx in range(SIDE) for dc in range(CORES) if dx or dc
+    )
+    column = tuple(at(x, y + dy, core) for dy in range(1, SIDE))
 
     def tell(semaphore, peers):
         for peer in peers:
@@ -131,12 +132,13 @@
 
     barrier = pltpu.get_barrier_semaphore()
     relayed = min(RELAYED, groups - 2)
+    handed = relayed + 1
 
     @pl.when(tm >= 1)
     def _():
         pl.semaphore_signal(barrier, inc=1, device_id=(tm - 1, tile), device_id_type=MESH)
 
-    @pl.when(tm >= relayed + 2)
+    @pl.when(tm >= handed + 2)
     def _():
         pl.semaphore_signal(barrier, inc=1, device_id=(tm - 2, tile), device_id_type=MESH)
 
@@ -144,22 +146,22 @@
     def _():
         pl.semaphore_signal(barrier, inc=1, device_id=(tm + 1, tile), device_id_type=MESH)
 
-    tell(barrier, beside_core + beside_x + beside_y)
 
     own = pltpu.make_async_copy(lat_in.at[0], lat.at[4:6], load_sem.at[0])
     own.start()
-    chunks = []
-
-    def load_chunk(k):
+
+    def chunk(k):
         rows = slice(k * C_MID, (k + 1) * C_MID)
-        chunk = []
-        for lag in range(3):
-            copy = pltpu.make_async_copy(
+        return [
+            pltpu.make_async_copy(
                 mid_w_in.at[lag, rows], w_mid.at[lag, rows], chunk_sem.at[3 * k + lag]
             )
-            copy.start()
-            chunk.append(copy)
-        chunks.append(chunk)
+            for lag in range(3)
+        ]
+
+    def load_chunk(k):
+        for copy in chunk(k):
+            copy.start(priority=1)
 
     load_chunk(0)
     loads = []
@@ -181,9 +183,12 @@
     for k in range(1, 9):
         load_chunk(k)
 
+    tell(barrier, row + column)
+
+
     def halo(d):
         return remote(
-            lat_in.at[0],
+            lat.at[4:6],
             lat.at[4 - 2 * d : 6 - 2 * d],
             halo_send.at[d - 1],
             halo_recv.at[d - 1],
@@ -191,8 +196,18 @@
             tile,
         )
 
+    def hand_on():
+        return remote(
+            lat.at[2:4],
+            lat.at[0:2],
+            halo_send.at[2],
+            halo_recv.at[1],
+            lax.rem(tm + 1, groups),
+            tile,
+        )
+
     def mix_weights(k):
-        for copy in chunks[k]:
+        for copy in chunk(k):
             copy.wait()
 
         @pl.loop(0, C_MID // 64)
@@ -205,13 +220,17 @@
 
     own.wait()
     spread_columns(cols, lat, 4, 2)
-    for k in range(2):
-        mix_weights(k)
+    mix_weights(0)
+
+    @pl.when(tm == handed)
+    def _():
+        for k in range(1, 6):
+            mix_weights(k)
 
     expected = (
-        5
+        len(row + column)
         + (tm < groups - 1).astype(jnp.int32)
-        + jnp.logical_and(tm >= relayed, tm < groups - 2).astype(jnp.int32)
+        + jnp.logical_and(tm >= handed, tm < groups - 2).astype(jnp.int32)
         + jnp.logical_and(tm >= 1, tm <= relayed).astype(jnp.int32)
     )
     pl.semaphore_wait(barrier, expected)
@@ -220,7 +239,7 @@
     def _():
         halo(1).start()
 
-    @pl.when(jnp.logical_and(tm >= relayed, tm < groups - 2))
+    @pl.when(jnp.logical_and(tm >= handed, tm < groups - 2))
     def _():
         halo(2).start()
 
@@ -228,13 +247,19 @@
     def _():
         pl.semaphore_signal(after, inc=1, device_id=(tm - 1, tile), device_id_type=MESH)
 
-    tell(hop.at[0], beside_core)
-    for k in range(2, 7):
-        mix_weights(k)
-    pl.semaphore_wait(hop.at[0], 1)
-    tell(hop.at[1], beside_x)
-
-    for k in range(7, 9):
+    tell(hop, column)
+
+    @pl.when(tm != handed)
+    def _():
+        for k in range(1, 6):
+            mix_weights(k)
+
+    @pl.when(tm == handed)
+    def _():
+        halo(1).wait_recv()
+        hand_on().start()
+
+    for k in range(6, 9):
         mix_weights(k)
     for copy in loads:
         copy.wait()
@@ -264,12 +289,9 @@
         v[i, 0:TW, :] = m[0:TW]
         v[i, TW + PIX : 2 * TW + PIX, :] = m[PIX - TW : PIX]
 
-    @pl.when(tm >= 1)
+    @pl.when(jnp.logical_and(tm >= 1, tm != handed))
     def _():
         halo(1).wait_recv()
-
-    pl.semaphore_wait(hop.at[1], 2)
-    tell(hop.at[2], beside_x)
 
     @pl.when(tm == 0)
     def _():
@@ -283,9 +305,6 @@
     @pl.when(tm >= 2)
     def _():
         halo(2).wait_recv()
-
-    pl.semaphore_wait(hop.at[2], 2)
-    tell(hop.at[3], beside_y)
 
     @pl.when(tm == 1)
     def _():
@@ -350,7 +369,7 @@
     )
     gather[tile] = jnp.concatenate([pixels[:, :128], pixels[:, 128:]], axis=0).astype(BF16)
 
-    pl.semaphore_wait(hop.at[3], 2)
+    pl.semaphore_wait(hop, len(column))
     for dx, dy, dc in FAR_FIRST:
         to = at(x + dx, y + dy, core + dc)
         remote(gather.at[tile], gather.at[tile], all_send, all_recv, tm, to).start()
@@ -398,11 +417,18 @@
     for c in range(3):
         blended[0, c] = mix[2 * c : 2 * c + 2]
     everyone.wait_send()
-    for d in (1, 2):
-
-        @pl.when(tm < groups - d)
-        def _():
-            halo(d).wait_send()
+
+    @pl.when(tm < groups - 1)
+    def _():
+        halo(1).wait_send()
+
+    @pl.when(jnp.logical_and(tm != relayed, tm < groups - 2))
+    def _():
+        halo(2).wait_send()
+
+    @pl.when(tm == handed)
+    def _():
+        hand_on().wait_send()
 
 
 def copy_kernel(written_in, blended_in, written_out, blended_out, sem):
@@ -463,13 +489,13 @@
             pltpu.SMEM((tiles,), jnp.int32),
             pltpu.SMEM((1,), jnp.int32),
             pltpu.SMEM((3,), F32),
-            pltpu.SemaphoreType.DMA((2,)),
+            pltpu.SemaphoreType.DMA((3,)),
             pltpu.SemaphoreType.DMA((2,)),
             pltpu.SemaphoreType.DMA,
             pltpu.SemaphoreType.DMA,
             pltpu.SemaphoreType.DMA((9,)),
             pltpu.SemaphoreType.DMA((27,)),
-            pltpu.SemaphoreType.REGULAR((4,)),
+            pltpu.SemaphoreType.REGULAR,
             pltpu.SemaphoreType.REGULAR,
         ],
         compiler_params=pltpu.CompilerParams(

time: 21.1 us -> 19.9 us (0.943); the launches traced: 20.8 us -> 19.8 us
  Pallas kernels: 19.5 us -> 18.5 us
    pallas_call x1, Pallas kernels: 18.8 us -> 17.9 us  [per_device(): pl.pallas_call(body, out_shape=tuple((pltpu.VMEM(s.shape, s.dtype) for s...]
where the time goes in v3:
time: 19.9 us; the launch traced here: 19.8 us
  Pallas kernels  18.5 us (93%)
  between operations  1.29 us (6%)
    pallas_call x1, Pallas kernels, per_device(): pl.pallas_call(body, out_shape=tuple((pltpu.VMEM(s.shape, s.dtype) for s...  17.9 us
    pallas_call x1, Pallas kernels, per_device(): pl.pallas_call(copy_kernel, out_shape=shapes, in_specs=[anywhere] * 2, ou...  0.62 us

profile of v3, /device:TPU:129, one launch (start us, length us, event | category | flops | bytes accessed | tf_op | source)
XLA Modules:
  0.0 19.8 jit_solution(13660666294973574638)
XLA Ops:
  1.3 17.9 %decode.1 = (bf16[3,3,2,256]{3,2,1,0:T(2,128)(2,1)S(1)}, bf16[1,3,2,256]{3,2,1,0:T(2,128)(2,1)S(1)}) custom-call(bf16[1,2,16,256]{3,2,1,0:T(8,128)(2,1)} %refs_0_.1, s32[32]{0:T(128)} %refs_1_.1, s32[1]{0:T(128)S(6)} %copy.12.refs_2_, bf16[3,144,512]{2,1,0:T(8,128)(2,1)} %refs_3_.1, f32[1,512]{1,0:T(1,128)} %bitcast.5, bf16[3,4608,256]{2,1,0:T(8,128)(2,1)} %refs_5_.1, ...), custom_call_target="tpu_custom_call" | custom-call | tf_op jit(solution)/shard_map/decode/pallas_call | solution.py:469
  19.2 0.6 %hand_out.1 = (bf16[3,3,2,256]{3,2,1,0:T(2,128)(2,1)}, bf16[1,3,2,256]{3,2,1,0:T(2,128)(2,1)}) custom-call(bf16[3,3,2,256]{3,2,1,0:T(2,128)(2,1)S(1)} %get-tuple-element.6.written_in, bf16[1,3,2,256]{3,2,1,0:T(2,128)(2,1)S(1)} %get-tuple-element.7.blended_in), custom_call_target="tpu_custom_call" | custom-call | tf_op jit(solution)/shard_map/hand_out/pallas_call | solution.py:522

commit v4 on v3

--- a/solution.py
+++ b/solution.py
@@ -19,6 +19,11 @@
 CORES = 2
 MESH = pl.DeviceIdType.MESH
 RELAYED = 2
+PAIRS = TH // 2
+HALF = PIX // 2
+STEP = 16
+PARTS = ((0, 0, C_MID), (1, 0, C_MID), (2, 0, C_MID // 2), (2, C_MID // 2, C_MID // 2))
+MIXED = tuple((i, r) for i in range(4) for r in range(4) if i in (1, 2) or r in (1, 2))
 FAR_FIRST = sorted(
     (
         (dx, dy, dc)
@@ -67,7 +72,7 @@
 def shift_rows(z, in_row, step):
     if step < 0:
         return jnp.where(in_row == 0, z, pltpu.roll(z, 1, 0))
-    return jnp.where(in_row == TW - 1, z, pltpu.roll(z, PIX - 1, 0))
+    return jnp.where(in_row == TW - 1, z, pltpu.roll(z, HALF - 1, 0))
 
 
 def decode_kernel(
@@ -97,6 +102,8 @@
     v,
     first_out,
     acc,
+    base,
+    terms,
     gated,
     gather,
     s_writer,
@@ -150,20 +157,26 @@
     own = pltpu.make_async_copy(lat_in.at[0], lat.at[4:6], load_sem.at[0])
     own.start()
 
-    def chunk(k):
-        rows = slice(k * C_MID, (k + 1) * C_MID)
-        return [
-            pltpu.make_async_copy(
-                mid_w_in.at[lag, rows], w_mid.at[lag, rows], chunk_sem.at[3 * k + lag]
-            )
-            for lag in range(3)
-        ]
-
-    def load_chunk(k):
-        for copy in chunk(k):
+    def part(k):
+        column, first, count = PARTS[k]
+        copies = []
+        for a in range(3):
+            for lag in range(3):
+                rows = pl.ds((3 * a + column) * C_MID + first, count)
+                copies.append(
+                    pltpu.make_async_copy(
+                        mid_w_in.at[lag, rows],
+                        w_mid.at[lag, rows],
+                        chunk_sem.at[9 * k + 3 * a + lag],
+                    )
+                )
+        return copies
+
+    def load_part(k):
+        for copy in part(k):
             copy.start(priority=1)
 
-    load_chunk(0)
+    load_part(0)
     loads = []
     for k, (src, dst) in enumerate(
         (
@@ -180,8 +193,8 @@
         copy = pltpu.make_async_copy(src, dst, load_sem.at[k + 1])
         copy.start()
         loads.append(copy)
-    for k in range(1, 9):
-        load_chunk(k)
+    for k in range(1, 4):
+        load_part(k)
 
     tell(barrier, row + column)
 
@@ -206,25 +219,34 @@
             tile,
         )
 
+    def mix(first, second, third):
+        even = first + third
+        return first, even + second, even - second, third
+
     def mix_weights(k):
-        for copy in chunk(k):
+        for copy in part(k):
             copy.wait()
-
-        @pl.loop(0, C_MID // 64)
+        column, first, count = PARTS[k]
+
+        @pl.loop(0, count // STEP)
         def _(s):
-            rows = pl.ds(pl.multiple_of(k * C_MID + s * 64, 64), 64)
-            even = w_mid[0, rows, :].astype(F32) + w_mid[2, rows, :].astype(F32)
-            odd = w_mid[1, rows, :].astype(F32)
-            u[0, rows, :] = (even + odd).astype(BF16)
-            u[1, rows, :] = (even - odd).astype(BF16)
+            at_row = first + s * STEP
+            by_row = []
+            for a in range(3):
+                rows = pl.ds(pl.multiple_of((3 * a + column) * C_MID + at_row, STEP), STEP)
+                by_row.append(mix(*(w_mid[lag, rows, :].astype(F32) for lag in range(3))))
+            rows = pl.ds(pl.multiple_of(column * C_MID + at_row, STEP), STEP)
+            for i in range(4):
+                by_time = mix(*(by_row[a][i] for a in range(3)))
+                for r in range(4):
+                    if (i, r) in MIXED:
+                        u[MIXED.index((i, r)), rows, :] = by_time[r].astype(BF16)
 
     own.wait()
     spread_columns(cols, lat, 4, 2)
-    mix_weights(0)
-
     @pl.when(tm == handed)
     def _():
-        for k in range(1, 6):
+        for k in range(2):
             mix_weights(k)
 
     expected = (
@@ -251,7 +273,7 @@
 
     @pl.when(tm != handed)
     def _():
-        for k in range(1, 6):
+        for k in range(2):
             mix_weights(k)
 
     @pl.when(tm == handed)
@@ -259,7 +281,7 @@
         halo(1).wait_recv()
         hand_on().start()
 
-    for k in range(6, 9):
+    for k in range(2, 4):
         mix_weights(k)
     for copy in loads:
         copy.wait()
@@ -280,14 +302,19 @@
         )
         out = (out + b_in[...]).astype(BF16)
         if j >= 2:
-            first_out[j - 2] = out
+            by_pair = out.reshape(PAIRS, 2, TW, C_MID)
+            for p in range(2):
+                first_out[j - 2, p] = by_pair[:, p].reshape(HALF, C_MID)
         return silu(out.astype(F32))
 
     def keep(i, m):
-        m = m.astype(BF16)
-        v[i, TW : TW + PIX, :] = m
-        v[i, 0:TW, :] = m[0:TW]
-        v[i, TW + PIX : 2 * TW + PIX, :] = m[PIX - TW : PIX]
+        by_pair = m.reshape(PAIRS, 2, TW, C_MID)
+        upper, lower = by_pair[:, 0], by_pair[:, 1]
+        above = jnp.concatenate([upper[:1], lower[:-1]], axis=0)
+        below = jnp.concatenate([upper[1:], lower[-1:]], axis=0)
+        rows = (above - lower, 0.5 * (upper + lower), 0.5 * (lower - upper), upper - below)
+        for r in range(4):
+            v[4 * i + r] = rows[r].reshape(HALF, C_MID).astype(BF16)
 
     @pl.when(jnp.logical_and(tm >= 1, tm != handed))
     def _():
@@ -301,6 +328,9 @@
     spread_columns(cols, lat, 2, 2)
     act2 = features(2)
     act3 = features(3)
+    for f in range(2):
+        for p in range(2):
+            base[f, p] = jnp.dot(first_out[f, p], w_skip[...], preferred_element_type=F32) + b_mid[...]
 
     @pl.when(tm >= 2)
     def _():
@@ -318,38 +348,40 @@
     keep(3, act1 - act3)
     keep(0, features(0) - act2)
 
-    in_row = lax.broadcasted_iota(jnp.int32, (PIX, C_OUT), 0) % TW
-
-    def product(i, e):
-        frames, weights = [], []
-        for r in range(3):
-            rows = slice((3 * r + e) * C_MID, (3 * r + e + 1) * C_MID)
-            frames.append(v[i, TW * r : TW * r + PIX, :])
-            if i in (0, 3):
-                weights.append(w_mid[0 if i == 0 else 2, rows, :])
+    in_row = lax.broadcasted_iota(jnp.int32, (HALF, C_OUT), 0) % TW
+
+    def product(i, r, e):
+        if (i, r) in MIXED:
+            weights = u[MIXED.index((i, r)), e * C_MID : (e + 1) * C_MID, :]
+        else:
+            tap = 6 + e if r else e
+            weights = w_mid[2 if i else 0, tap * C_MID : (tap + 1) * C_MID, :]
+        return jnp.dot(v[4 * i + r], weights, preferred_element_type=F32)
+
+    def row_pair(i, e):
+        for r in range(4):
+            terms[i % 2, e, r] = product(i, r, e)
+        p = [terms[i % 2, e, r] for r in range(4)]
+        return p[0] + p[1] + p[2], p[1] - p[2] - p[3]
+
+    def finish(f, p, sums):
+        total = sums[1] + shift_rows(sums[0], in_row, -1) + shift_rows(sums[2], in_row, 1)
+        total = silu(total + base[f, p]).astype(BF16)
+        gated[:, p, :, f * C_OUT : (f + 1) * C_OUT] = total.reshape(PAIRS, TW, C_OUT)
+
+    for e in range(3):
+        first = row_pair(1, e)
+        second = row_pair(2, e)
+        for p in range(2):
+            acc[0, p, e] = first[p] + second[p]
+            acc[1, p, e] = first[p] - second[p]
+    for f, i in ((0, 0), (1, 3)):
+        last = [row_pair(i, e) for e in range(3)]
+        for p in range(2):
+            if f == 0:
+                finish(f, p, [acc[f, p, e] + last[e][p] for e in range(3)])
             else:
-                weights.append(u[i - 1, rows, :])
-        return jnp.dot(
-            jnp.concatenate(frames, axis=1),
-            jnp.concatenate(weights, axis=0),
-            preferred_element_type=F32,
-        )
-
-    def finish(f, sums):
-        total = sums[1] + shift_rows(sums[0], in_row, -1) + shift_rows(sums[2], in_row, 1)
-        total = total + jnp.dot(first_out[f], w_skip[...], preferred_element_type=F32) + b_mid[...]
-        gated[:, f * C_OUT : (f + 1) * C_OUT] = silu(total).astype(BF16)
-
-    for e in range(3):
-        p1 = product(1, e)
-        acc[0, e] = p1
-        acc[1, e] = p1
-    for e in range(3):
-        p2 = product(2, e)
-        acc[0, e] += p2
-        acc[1, e] -= p2
-    finish(0, [acc[0, e] + product(0, e) for e in range(3)])
-    finish(1, [acc[1, e] - product(3, e) for e in range(3)])
+                finish(f, p, [acc[f, p, e] - last[e][p] for e in range(3)])
 
     row = lax.broadcasted_iota(jnp.int32, (8, C_OUT), 0)
     head = w_head[...].astype(F32)
@@ -362,7 +394,7 @@
         [jnp.where(row % 2 == 0, by_color, 0.0), jnp.where(row % 2 == 1, by_color, 0.0)], axis=1
     ).astype(BF16)
     pixels = lax.dot_general(
-        head2, gated[...], (((1,), (1,)), ((), ())), preferred_element_type=F32
+        head2, gated[...].reshape(PIX, 2 * C_OUT), (((1,), (1,)), ((), ())), preferred_element_type=F32
     )
     pixels = pixels + jnp.where(
         row // 2 == 0, s_head_b[0], jnp.where(row // 2 == 1, s_head_b[1], s_head_b[2])
@@ -480,11 +512,13 @@
             pltpu.VMEM((1, C_OUT), F32),
             pltpu.VMEM((C_MID, C_OUT), BF16),
             pltpu.VMEM((3, C_OUT), BF16),
-            pltpu.VMEM((2, 9 * C_MID, C_OUT), BF16),
-            pltpu.VMEM((4, PIX + 2 * TW, C_MID), BF16),
-            pltpu.VMEM((2, PIX, C_MID), BF16),
-            pltpu.VMEM((2, 3, PIX, C_OUT), F32),
-            pltpu.VMEM((PIX, 2 * C_OUT), BF16),
+            pltpu.VMEM((len(MIXED), 3 * C_MID, C_OUT), BF16),
+            pltpu.VMEM((16, HALF, C_MID), BF16),
+            pltpu.VMEM((2, 2, HALF, C_MID), BF16),
+            pltpu.VMEM((2, 2, 3, HALF, C_OUT), F32),
+            pltpu.VMEM((2, 2, HALF, C_OUT), F32),
+            pltpu.VMEM((2, 3, 4, HALF, C_OUT), F32),
+            pltpu.VMEM((PAIRS, 2, TW, 2 * C_OUT), BF16),
             pltpu.VMEM((tiles, 16, 128), BF16),
             pltpu.SMEM((tiles,), jnp.int32),
             pltpu.SMEM((1,), jnp.int32),
@@ -494,7 +528,7 @@
             pltpu.SemaphoreType.DMA,
             pltpu.SemaphoreType.DMA,
             pltpu.SemaphoreType.DMA((9,)),
-            pltpu.SemaphoreType.DMA((27,)),
+            pltpu.SemaphoreType.DMA((36,)),
             pltpu.SemaphoreType.REGULAR,
             pltpu.SemaphoreType.REGULAR,
         ],

time: 19.9 us -> 19.5 us (0.980)
  Pallas kernels: 18.5 us -> 18.2 us
    pallas_call x1, Pallas kernels: 17.9 us -> 17.5 us  [per_device(): pl.pallas_call(body, out_shape=tuple((pltpu.VMEM(s.shape, s.dtype) for s...]
where the time goes in v4:
time: 19.5 us; the launch traced here: 19.4 us
  Pallas kernels  18.2 us (93%)
  between operations  1.29 us (7%)
    pallas_call x1, Pallas kernels, per_device(): pl.pallas_call(body, out_shape=tuple((pltpu.VMEM(s.shape, s.dtype) for s...  17.5 us
    pallas_call x1, Pallas kernels, per_device(): pl.pallas_call(copy_kernel, out_shape=shapes, in_specs=[anywhere] * 2, ou...  0.62 us

profile of v4, /device:TPU:129, one launch (start us, length us, event | category | flops | bytes accessed | tf_op | source)
XLA Modules:
  0.0 19.4 jit_solution(16179217603777813108)
XLA Ops:
  1.3 17.5 %decode.1 = (bf16[3,3,2,256]{3,2,1,0:T(2,128)(2,1)S(1)}, bf16[1,3,2,256]{3,2,1,0:T(2,128)(2,1)S(1)}) custom-call(bf16[1,2,16,256]{3,2,1,0:T(8,128)(2,1)} %refs_0_.1, s32[32]{0:T(128)} %refs_1_.1, s32[1]{0:T(128)S(6)} %copy.12.refs_2_, bf16[3,144,512]{2,1,0:T(8,128)(2,1)} %refs_3_.1, f32[1,512]{1,0:T(1,128)} %bitcast.5, bf16[3,4608,256]{2,1,0:T(8,128)(2,1)} %refs_5_.1, ...), custom_call_target="tpu_custom_call" | custom-call | tf_op jit(solution)/shard_map/decode/pallas_call | solution.py:501
  18.8 0.6 %hand_out.1 = (bf16[3,3,2,256]{3,2,1,0:T(2,128)(2,1)}, bf16[1,3,2,256]{3,2,1,0:T(2,128)(2,1)}) custom-call(bf16[3,3,2,256]{3,2,1,0:T(2,128)(2,1)S(1)} %get-tuple-element.6.written_in, bf16[1,3,2,256]{3,2,1,0:T(2,128)(2,1)S(1)} %get-tuple-element.7.blended_in), custom_call_target="tpu_custom_call" | custom-call | tf_op jit(solution)/shard_map/hand_out/pallas_call | solution.py:556

commit v5 on v4

--- a/solution.py
+++ b/solution.py
@@ -21,7 +21,7 @@
 RELAYED = 2
 PAIRS = TH // 2
 HALF = PIX // 2
-STEP = 16
+STEP = 32
 PARTS = ((0, 0, C_MID), (1, 0, C_MID), (2, 0, C_MID // 2), (2, C_MID // 2, C_MID // 2))
 MIXED = tuple((i, r) for i in range(4) for r in range(4) if i in (1, 2) or r in (1, 2))
 FAR_FIRST = sorted(
@@ -291,6 +291,17 @@
         pl.semaphore_wait(after, 1)
         halo(2).start()
 
+    row = lax.broadcasted_iota(jnp.int32, (8, C_OUT), 0)
+    head = w_head[...].astype(F32)
+    by_color = jnp.where(
+        row // 2 == 0,
+        head[0:1],
+        jnp.where(row // 2 == 1, head[1:2], jnp.where(row // 2 == 2, head[2:3], 0.0)),
+    )
+    head2 = jnp.concatenate(
+        [jnp.where(row % 2 == 0, by_color, 0.0), jnp.where(row % 2 == 1, by_color, 0.0)], axis=1
+    ).astype(BF16)
+
     weight = w_in[...].reshape(3 * TAPS, C_MID)
 
     def features(j):
@@ -383,16 +394,6 @@
             else:
                 finish(f, p, [acc[f, p, e] - last[e][p] for e in range(3)])
 
-    row = lax.broadcasted_iota(jnp.int32, (8, C_OUT), 0)
-    head = w_head[...].astype(F32)
-    by_color = jnp.where(
-        row // 2 == 0,
-        head[0:1],
-        jnp.where(row // 2 == 1, head[1:2], jnp.where(row // 2 == 2, head[2:3], 0.0)),
-    )
-    head2 = jnp.concatenate(
-        [jnp.where(row % 2 == 0, by_color, 0.0), jnp.where(row % 2 == 1, by_color, 0.0)], axis=1
-    ).astype(BF16)
     pixels = lax.dot_general(
         head2, gated[...].reshape(PIX, 2 * C_OUT), (((1,), (1,)), ((), ())), preferred_element_type=F32
     )

time: 19.5 us -> 19.6 us (level)
  no operation moved by 1% of the time
where the time goes in v5:
time: 19.6 us; the launch traced here: 19.5 us
  Pallas kernels  18.2 us (93%)
  between operations  1.29 us (7%)
    pallas_call x1, Pallas kernels, per_device(): pl.pallas_call(body, out_shape=tuple((pltpu.VMEM(s.shape, s.dtype) for s...  17.6 us
    pallas_call x1, Pallas kernels, per_device(): pl.pallas_call(copy_kernel, out_shape=shapes, in_specs=[anywhere] * 2, ou...  0.62 us

profile of v5, /device:TPU:129, one launch (start us, length us, event | category | flops | bytes accessed | tf_op | source)
XLA Modules:
  0.0 19.5 jit_solution(11814100784556162676)
XLA Ops:
  1.3 17.6 %decode.1 = (bf16[3,3,2,256]{3,2,1,0:T(2,128)(2,1)S(1)}, bf16[1,3,2,256]{3,2,1,0:T(2,128)(2,1)S(1)}) custom-call(bf16[1,2,16,256]{3,2,1,0:T(8,128)(2,1)} %refs_0_.1, s32[32]{0:T(128)} %refs_1_.1, s32[1]{0:T(128)S(6)} %copy.12.refs_2_, bf16[3,144,512]{2,1,0:T(8,128)(2,1)} %refs_3_.1, f32[1,512]{1,0:T(1,128)} %bitcast.5, bf16[3,4608,256]{2,1,0:T(8,128)(2,1)} %refs_5_.1, ...), custom_call_target="tpu_custom_call" | custom-call | tf_op jit(solution)/shard_map/decode/pallas_call | solution.py:502
  18.8 0.6 %hand_out.1 = (bf16[3,3,2,256]{3,2,1,0:T(2,128)(2,1)}, bf16[1,3,2,256]{3,2,1,0:T(2,128)(2,1)}) custom-call(bf16[3,3,2,256]{3,2,1,0:T(2,128)(2,1)S(1)} %get-tuple-element.6.written_in, bf16[1,3,2,256]{3,2,1,0:T(2,128)(2,1)S(1)} %get-tuple-element.7.blended_in), custom_call_target="tpu_custom_call" | custom-call | tf_op jit(solution)/shard_map/hand_out/pallas_call | solution.py:557
